TPU v7x, 32 devices: a whole 2x2x4 slice. The times are simulated.
32 devices in a mesh: fib: 4 (over y, x), rest: 8 (over z, core).
Axes of the slice: x: 2, y: 2, z: 4, core: 2. Of those that a mesh axis runs over, the one named last changes fastest.
Arguments:
- tensor: float32 [32, 32, 64, 1024], P('fib', 'rest'), may hold values from -24 to 24
- factor_one: float32 [1024, 128], replicated, may hold values from 0 to 0.05
- factor_two: float32 [32, 128], P('fib'), may hold values from 0.05 to 0.35
- factor_three: float32 [32, 128], P('rest'), may hold values from 0.03 to 0.25
- factor_four: float32 [64, 128], replicated, may hold values from 0.03 to 0.25
Outputs:
- new_factor: float32 [1024, 128], replicated
- factor_gram: float32 [128, 128], replicated
All inputs are finite; a program needn't handle non-finite values.
Results may differ from a plain program's by a relative error of at most 0.00014.
Values sent between devices are 32-bit elements; how exact they have to be, the bound alone decides.
A program may use at most 64 MiB of HBM per device.

v0:
```python
import functools

import jax
import jax.numpy as jnp
from jax import lax
from jax.experimental import pallas as pl
from jax.experimental.pallas import tpu as pltpu
from jax.sharding import PartitionSpec as P

MESH = pl.DeviceIdType.MESH
HIGHEST = lax.Precision.HIGHEST
LANES = 128
BLOCK = 8


def split_bf16(value):
    high = value.astype(jnp.bfloat16)
    low = (value - high.astype(jnp.float32)).astype(jnp.bfloat16)
    return high, low


def gram_of(rows):
    return lax.dot_general(
        rows, rows, (((0,), (0,)), ((), ())),
        precision=HIGHEST, preferred_element_type=jnp.float32,
    )


def kernel(
    cfg, tensor, factor_one, factor_two, factor_three, factor_four, out,
    tbuf, xown, khatri_t, two_all, three_all, three_cat, part, recv_core, sum_core,
    recv_fib, sum_fib, recv_z, mine, scaled, spread, fresh, four_held, held,
    factor_sem, store_sem, tensor_sem, xown_sem, two_send, two_recv, three_send, three_recv,
    core_send, core_recv, fib_send, fib_recv, z_send, z_recv,
    gz_send, gz_recv, gf_send, gf_recv, gc_send, gc_recv,
):
    nfib, nrest, nz, chunks, piece = cfg
    rank = factor_two.shape[1]
    fib = lax.axis_index("fib")
    rest = lax.axis_index("rest")
    core = rest % 2
    z = rest // 2
    other = 1 - core
    width = tensor.shape[1] // chunks
    pieces = nfib * nz
    nblocks = rank // BLOCK

    def remote(src, dst, send, recv, fib_to, rest_to):
        return pltpu.make_async_remote_copy(
            src_ref=src, dst_ref=dst, send_sem=send, recv_sem=recv,
            device_id=(fib_to, rest_to), device_id_type=MESH,
        )

    factor_loads = [
        pltpu.make_async_copy(factor_two, two_all.at[fib], factor_sem.at[0]),
        pltpu.make_async_copy(factor_three, three_all.at[rest], factor_sem.at[1]),
        pltpu.make_async_copy(factor_four, four_held, factor_sem.at[2]),
    ]
    for copy in factor_loads:
        copy.start()
    loads = []
    for chunk in range(chunks):
        copy = pltpu.make_async_copy(
            tensor.at[:, pl.ds(chunk * width, width)], tbuf.at[chunk], tensor_sem.at[chunk]
        )
        loads.append(copy)
    for copy in loads[:2]:
        copy.start()
    barrier = pltpu.get_barrier_semaphore()
    for d in range(1, nfib):
        pl.semaphore_signal(barrier, inc=1, device_id=((fib + d) % nfib, rest), device_id_type=MESH)
    for d in range(1, nrest):
        pl.semaphore_signal(barrier, inc=1, device_id=(fib, (rest + d) % nrest), device_id_type=MESH)

    xown_copy = pltpu.make_async_copy(factor_one.at[:, core, fib, z], xown, xown_sem)
    xown_copy.start()

    for copy in factor_loads:
        copy.wait()

    two = two_all[fib]
    three = three_all[rest]
    four = four_held[...]
    rows_two, rows_three, rows_four = two.shape[0], three.shape[0], four.shape[0]
    for i2 in range(rows_two):
        tile = jnp.concatenate(
            [(two[i2 : i2 + 1] * three[i3 : i3 + 1]) * four for i3 in range(rows_three)], axis=0
        )
        high, low = split_bf16(tile.T)
        span = rows_three * rows_four
        khatri_t[0:rank, i2 * span : (i2 + 1) * span] = high
        khatri_t[rank : 2 * rank, i2 * span : (i2 + 1) * span] = low

    small = []
    for d in range(1, nfib):
        small.append(remote(two_all.at[fib], two_all.at[fib], two_send.at[d], two_recv.at[d], (fib + d) % nfib, rest))
    for d in range(1, nrest):
        small.append(remote(three_all.at[rest], three_all.at[rest], three_send.at[d], three_recv.at[d], fib, (rest + d) % nrest))

    sends = list(small)

    def multiply(chunk):
        loads[chunk].wait()
        if chunk + 2 < chunks:
            loads[chunk + 2].start()
        depth = tbuf.shape[1]
        step = min(depth, 512)
        total = None
        for k in range(0, depth, step):
            high, low = split_bf16(tbuf[chunk, k : k + step, :])
            weights = khatri_t[:, k : k + step]
            term = jnp.dot(weights, high, preferred_element_type=jnp.float32)
            term = term + jnp.dot(weights, low, preferred_element_type=jnp.float32)
            total = term if total is None else total + term
        value = (total[0:rank] + total[rank : 2 * rank]).T
        if piece % 8 == 0:
            part[chunk] = value.reshape(2 * pieces, piece, rank)
        else:
            for p in range(2 * pieces):
                part[chunk, p] = value[p * piece : (p + 1) * piece]

    core_copies, fib_copies, z_copies = {}, {}, {}

    def start_core(chunk):
        copy = remote(
            part.at[chunk, pl.ds(other * pieces, pieces)], recv_core.at[chunk],
            core_send.at[chunk], core_recv.at[chunk], fib, z * 2 + other,
        )
        copy.start()
        core_copies[chunk] = copy
        sends.append(copy)

    def start_fib(chunk):
        core_copies[chunk].wait_recv()
        sum_core[chunk] = part[chunk, pl.ds(core * pieces, pieces)] + recv_core[chunk]
        fib_copies[chunk] = []
        for d in range(1, nfib):
            to = (fib + d) % nfib
            copy = remote(
                sum_core.at[chunk, pl.ds(to * nz, nz)], recv_fib.at[chunk, d - 1],
                fib_send.at[chunk, d], fib_recv.at[chunk, d], to, rest,
            )
            copy.start()
            fib_copies[chunk].append(copy)
            sends.append(copy)

    def start_z(chunk):
        total = sum_core[chunk, pl.ds(fib * nz, nz)]
        for d in range(1, nfib):
            fib_copies[chunk][d - 1].wait_recv()
            total = total + recv_fib[chunk, d - 1]
        sum_fib[chunk] = total
        z_copies[chunk] = []
        for d in range(1, nz):
            to = (z + d) % nz
            copy = remote(
                sum_fib.at[chunk, to], recv_z.at[chunk, d - 1],
                z_send.at[chunk, d], z_recv.at[chunk, d], fib, to * 2 + core,
            )
            copy.start()
            z_copies[chunk].append(copy)
            sends.append(copy)

    def finish(chunk):
        total = sum_fib[chunk, z]
        for d in range(1, nz):
            z_copies[chunk][d - 1].wait_recv()
            total = total + recv_z[chunk, d - 1]
        mine[chunk * piece : (chunk + 1) * piece, :] = total

    mine[...] = jnp.zeros_like(mine)
    fresh[...] = jnp.zeros_like(fresh)
    for chunk in range(chunks):
        multiply(chunk)
        if chunk == 0:
            pl.semaphore_wait(barrier, nfib - 1 + nrest - 1)
        start_core(chunk)
        if chunk == 0:
            for copy in small:
                copy.start()
        if chunk >= 1:
            start_fib(chunk - 1)
        if chunk >= 2:
            start_z(chunk - 2)

    for copy in small:
        copy.wait_recv()
    if rows_two % 8 == 0:
        all_two = two_all[...].reshape(nfib * rows_two, rank)
    else:
        all_two = jnp.concatenate([two_all[f] for f in range(nfib)], axis=0)
    for q in range(nrest):
        three_cat[q * rows_three : (q + 1) * rows_three, :] = three_all[q]
    gram_v = gram_of(all_two) * gram_of(three_cat[...]) * gram_of(four)
    row_of = lax.broadcasted_iota(jnp.int32, (rank, rank), 0)
    col_of = lax.broadcasted_iota(jnp.int32, (rank, rank), 1)
    diag = jnp.sum(jnp.where(row_of == col_of, gram_v, 0.0), axis=1, keepdims=True)
    inverse = 1.0 / diag
    upper = jnp.where(col_of > row_of, gram_v, 0.0)
    scaled[...] = gram_v * inverse

    if chunks >= 2:
        start_z(chunks - 2)
    start_fib(chunks - 1)

    for i in range(rank):
        low_row = (i // BLOCK) * BLOCK
        spread[i, low_row:rank, :] = jnp.broadcast_to(scaled[low_row:rank, i : i + 1], (rank - low_row, LANES))

    start_z(chunks - 1)
    xown_copy.wait()
    for chunk in range(chunks):
        fresh[chunk * piece : (chunk + 1) * piece, :] = xown[chunk]
    old_part = lax.dot_general(
        upper, fresh[...], (((1,), (1,)), ((), ())),
        precision=HIGHEST, preferred_element_type=jnp.float32,
    )

    for chunk in range(chunks):
        finish(chunk)

    start = (mine[...].T - old_part) * inverse
    state = [start[b * BLOCK : (b + 1) * BLOCK] for b in range(nblocks)]
    for b in range(nblocks):
        rows = [jnp.broadcast_to(state[b][k : k + 1], (BLOCK, LANES)) for k in range(BLOCK)]
        for k in range(BLOCK):
            i = b * BLOCK + k
            rows[k] = jnp.maximum(rows[k], 0.0)
            for later in range(k + 1, BLOCK):
                j = b * BLOCK + later
                ratio = jnp.broadcast_to(spread[i, j : j + 1, :], (BLOCK, LANES))
                rows[later] = rows[later] - ratio * rows[k]
            fresh[i : i + 1, :] = rows[k][0:1]
            for later in range(b + 1, nblocks):
                state[later] = state[later] - spread[i, later * BLOCK : (later + 1) * BLOCK, :] * rows[k]
    own_rows = fresh[...].T
    for chunk in range(chunks):
        held[chunk, fib, z] = own_rows[chunk * piece : (chunk + 1) * piece]

    reduce_sends = list(sends)
    sends.clear()

    z_gather = []
    for d in range(1, nz):
        to = (z + d) % nz
        ref = held.at[:, fib, z]
        copy = remote(ref, ref, gz_send.at[d], gz_recv.at[d], fib, to * 2 + core)
        copy.start()
        z_gather.append(copy)
        sends.append(copy)
    fib_gather = []
    for dz in range(nz):
        if dz:
            z_gather[dz - 1].wait_recv()
        at = (z + nz - dz) % nz
        group = []
        for d in range(1, nfib):
            ref = held.at[:, fib, at]
            copy = remote(ref, ref, gf_send.at[dz, d], gf_recv.at[dz, d], (fib + d) % nfib, rest)
            copy.start()
            group.append(copy)
            sends.append(copy)
        fib_gather.append(group)
    core_gather, stores = [], []
    for dz in range(nz):
        for copy in fib_gather[dz]:
            copy.wait_recv()
        at = (z + nz - dz) % nz
        copy = remote(
            held.at[:, :, at], out.at[:, core, :, at], gc_send.at[dz], gc_recv.at[dz], fib, z * 2 + other
        )
        copy.start()
        core_gather.append(copy)
        sends.append(copy)
        store = pltpu.make_async_copy(held.at[:, :, at], out.at[:, core, :, at], store_sem.at[dz])
        store.start()
        stores.append(store)
        if dz == 0:
            for copy in reduce_sends:
                copy.wait_send()

    for copy in stores:
        copy.wait()
    for copy in sends:
        copy.wait_send()
    for copy in core_gather:
        copy.wait_recv()


def results(gathered, new_factor, gram, held, load_sem, store_sem):
    parts = load_sem.shape[0]
    rows, rank = held.shape
    step = rows // parts
    loads, stores = [], []
    for k in range(parts):
        span = pl.ds(k * step, step)
        loads.append(pltpu.make_async_copy(gathered.at[span], held.at[span], load_sem.at[k]))
        stores.append(pltpu.make_async_copy(held.at[span], new_factor.at[span], store_sem.at[k]))
        loads[k].start()
    both = None
    for k in range(parts):
        loads[k].wait()
        stores[k].start()
        high, low = split_bf16(held[k * step : (k + 1) * step])
        term = lax.dot_general(
            high, jnp.concatenate([high, low], axis=1), (((0,), (0,)), ((), ())),
            preferred_element_type=jnp.float32,
        )
        both = term if both is None else both + term
    cross = both[:, rank:]
    gram[...] = both[:, :rank] + (cross + cross.T)
    for copy in stores:
        copy.wait()


def per_device(tensor, factor_one, factor_two, factor_three, factor_four):
    nfib, nrest = lax.axis_size("fib"), lax.axis_size("rest")
    nz = nrest // 2
    mode_one, rank = factor_one.shape
    own = mode_one // (nfib * nrest)
    chunks = 4 if own % 32 == 0 else 1
    piece = own // chunks
    pieces = nfib * nz
    depth = tensor.shape[0] * tensor.shape[1] * tensor.shape[2]
    flat = tensor.reshape(depth, mode_one)
    ordered = (chunks, 2, nfib, nz, piece, rank)
    f32, bf16 = jnp.float32, jnp.bfloat16
    vmem = pl.BlockSpec(memory_space=pltpu.VMEM)
    anywhere = pl.BlockSpec(memory_space=pl.ANY)
    dma = pltpu.SemaphoreType.DMA
    out = pl.pallas_call(
        functools.partial(kernel, (nfib, nrest, nz, chunks, piece)),
        out_shape=jax.ShapeDtypeStruct(ordered, f32),
        in_specs=[anywhere] * 5,
        out_specs=anywhere,
        scratch_shapes=[
            pltpu.VMEM((chunks, depth, mode_one // chunks), f32),
            pltpu.VMEM((chunks, piece, rank), f32),
            pltpu.VMEM((2 * rank, depth), bf16),
            pltpu.VMEM((nfib,) + factor_two.shape, f32),
            pltpu.VMEM((nrest,) + factor_three.shape, f32),
            pltpu.VMEM((nrest * factor_three.shape[0], rank), f32),
            pltpu.VMEM((chunks, 2 * pieces, piece, rank), f32),
            pltpu.VMEM((chunks, pieces, piece, rank), f32),
            pltpu.VMEM((chunks, pieces, piece, rank), f32),
            pltpu.VMEM((chunks, nfib - 1, nz, piece, rank), f32),
            pltpu.VMEM((chunks, nz, piece, rank), f32),
            pltpu.VMEM((chunks, nz - 1, piece, rank), f32),
            pltpu.VMEM((LANES, rank), f32),
            pltpu.VMEM((rank, rank), f32),
            pltpu.VMEM((rank, rank, LANES), f32),
            pltpu.VMEM((rank, LANES), f32),
            pltpu.VMEM(factor_four.shape, f32),
            pltpu.VMEM((chunks, nfib, nz, piece, rank), f32),
            dma((3,)), dma((nz,)),
            dma((chunks,)),
            dma,
            dma((nfib,)), dma((nfib,)),
            dma((nrest,)), dma((nrest,)),
            dma((chunks,)), dma((chunks,)),
            dma((chunks, nfib)), dma((chunks, nfib)),
            dma((chunks, nz)), dma((chunks, nz)),
            dma((nz,)), dma((nz,)),
            dma((nz, nfib)), dma((nz, nfib)),
            dma((nz,)), dma((nz,)),
        ],
        compiler_params=pltpu.CompilerParams(
            collective_id=0, has_side_effects=True, vmem_limit_bytes=56 * 1024 * 1024
        ),
    )(flat, factor_one.reshape(ordered), factor_two, factor_three, factor_four)
    return pl.pallas_call(
        results,
        out_shape=(
            jax.ShapeDtypeStruct((mode_one, rank), f32),
            jax.ShapeDtypeStruct((rank, rank), f32),
        ),
        in_specs=[anywhere],
        out_specs=(anywhere, vmem),
        scratch_shapes=[pltpu.VMEM((mode_one, rank), f32), dma((4,)), dma((4,))],
        compiler_params=pltpu.CompilerParams(vmem_limit_bytes=63 * 1024 * 1024),
    )(out.reshape(mode_one, rank))


def solution(mesh):
    return jax.shard_map(
        per_device,
        mesh=mesh,
        in_specs=(P("fib", "rest", None, None), P(), P("fib", None), P("rest", None), P()),
        out_specs=(P(), P()),
        check_vma=False,
    )
```

profile of v0, /device:TPU:0, one launch (start us, length us, event | category | flops | bytes accessed | tf_op | source)
XLA Modules:
  0.0 35.6 jit_solution(6925931858306929651)
XLA Ops:
  0.6 32.3 %shard_map.68 = f32[4,2,4,4,8,128]{5,4,3,2,1,0:T(8,128)} custom-call(f32[2048,1024]{1,0:T(8,128)} %bitcast.3, f32[4,2,4,4,8,128]{5,4,3,2,1,0:T(8,128)} %bitcast.5, f32[8,128]{1,0:T(8,128)} %factor_two.1, f32[4,128]{1,0:T(4,128)} %factor_three.1, f32[64,128]{1,0:T(8,128)} %factor_four.1), custom_call_target="tpu_custom_call" | custom-call | tf_op jit(solution)/shard_map/pallas_call | solution.py:331
  32.9 2.6 %shard_map.69 = (f32[1024,128]{1,0:T(8,128)}, f32[128,128]{1,0:T(8,128)}) custom-call(f32[1024,128]{1,0:T(8,128)} %bitcast.4), custom_call_target="tpu_custom_call" | custom-call | tf_op jit(solution)/shard_map/pallas_call | solution.py:371
where the time goes:
time: 35.7 us; the launch traced here: 35.6 us
  Pallas kernels  34.9 us (98%)
  between operations  0.64 us (2%)
    pallas_call x1, Pallas kernels, per_device(): pl.pallas_call(functools.partial(kernel, (nfib, nrest, nz, chunks, piece)...  32.3 us
    pallas_call x1, Pallas kernels, per_device(): pl.pallas_call(results, out_shape=(jax.ShapeDtypeStruct((mode_one, rank),...  2.65 us

commit v1 on v0

--- a/solution.py
+++ b/solution.py
@@ -29,7 +29,7 @@
 def kernel(
     cfg, tensor, factor_one, factor_two, factor_three, factor_four, out,
     tbuf, xown, khatri_t, two_all, three_all, three_cat, part, recv_core, sum_core,
-    recv_fib, sum_fib, recv_z, mine, scaled, spread, fresh, four_held, held,
+    recv_fib, sum_fib, recv_z, mine, scaled, spread, fresh, four_held, held, acc,
     factor_sem, store_sem, tensor_sem, xown_sem, two_send, two_recv, three_send, three_recv,
     core_send, core_recv, fib_send, fib_recv, z_send, z_recv,
     gz_send, gz_recv, gf_send, gf_recv, gc_send, gc_recv,
@@ -78,18 +78,23 @@
     for copy in factor_loads:
         copy.wait()
 
-    two = two_all[fib]
     three = three_all[rest]
     four = four_held[...]
-    rows_two, rows_three, rows_four = two.shape[0], three.shape[0], four.shape[0]
-    for i2 in range(rows_two):
+    rows_two, rows_three, rows_four = factor_two.shape[0], three.shape[0], four.shape[0]
+    span = rows_three * rows_four
+
+    def fill(i2, carry):
+        row = two_all[fib, pl.ds(i2, 1), :]
         tile = jnp.concatenate(
-            [(two[i2 : i2 + 1] * three[i3 : i3 + 1]) * four for i3 in range(rows_three)], axis=0
+            [(row * three[i3 : i3 + 1]) * four for i3 in range(rows_three)], axis=0
         )
         high, low = split_bf16(tile.T)
-        span = rows_three * rows_four
-        khatri_t[0:rank, i2 * span : (i2 + 1) * span] = high
-        khatri_t[rank : 2 * rank, i2 * span : (i2 + 1) * span] = low
+        at = pl.ds(pl.multiple_of(i2 * span, span), span)
+        khatri_t[0:rank, at] = high
+        khatri_t[rank : 2 * rank, at] = low
+        return carry
+
+    lax.fori_loop(0, rows_two, fill, 0)
 
     small = []
     for d in range(1, nfib):
@@ -105,13 +110,19 @@
             loads[chunk + 2].start()
         depth = tbuf.shape[1]
         step = min(depth, 512)
-        total = None
-        for k in range(0, depth, step):
-            high, low = split_bf16(tbuf[chunk, k : k + step, :])
-            weights = khatri_t[:, k : k + step]
+        acc[...] = jnp.zeros_like(acc)
+
+        def accumulate(k, carry):
+            at = pl.ds(pl.multiple_of(k * step, step), step)
+            high, low = split_bf16(tbuf[chunk, at, :])
+            weights = khatri_t[:, at]
             term = jnp.dot(weights, high, preferred_element_type=jnp.float32)
             term = term + jnp.dot(weights, low, preferred_element_type=jnp.float32)
-            total = term if total is None else total + term
+            acc[...] += term
+            return carry
+
+        lax.fori_loop(0, depth // step, accumulate, 0)
+        total = acc[...]
         value = (total[0:rank] + total[rank : 2 * rank]).T
         if piece % 8 == 0:
             part[chunk] = value.reshape(2 * pieces, piece, rank)
@@ -352,6 +363,7 @@
             pltpu.VMEM((rank, LANES), f32),
             pltpu.VMEM(factor_four.shape, f32),
             pltpu.VMEM((chunks, nfib, nz, piece, rank), f32),
+            pltpu.VMEM((2 * rank, mode_one // chunks), f32),
             dma((3,)), dma((nz,)),
             dma((chunks,)),
             dma,
@@ -376,7 +388,7 @@
         ),
         in_specs=[anywhere],
         out_specs=(anywhere, vmem),
-        scratch_shapes=[pltpu.VMEM((mode_one, rank), f32), dma((4,)), dma((4,))],
+        scratch_shapes=[pltpu.VMEM((mode_one, rank), f32), dma((1,)), dma((1,))],
         compiler_params=pltpu.CompilerParams(vmem_limit_bytes=63 * 1024 * 1024),
     )(out.reshape(mode_one, rank))
 

time: 35.7 us -> 35.8 us (level)
  no operation moved by 1% of the time
where the time goes in v1:
time: 35.8 us; the launch traced here: 35.6 us
  Pallas kernels  35 us (98%)
  between operations  0.64 us (2%)
    pallas_call x1, Pallas kernels, per_device(): pl.pallas_call(functools.partial(kernel, (nfib, nrest, nz, chunks, piece)...  32.5 us
    pallas_call x1, Pallas kernels, per_device(): pl.pallas_call(results, out_shape=(jax.ShapeDtypeStruct((mode_one, rank),...  2.48 us

profile of v1, /device:TPU:0, one launch (start us, length us, event | category | flops | bytes accessed | tf_op | source)
XLA Modules:
  0.0 35.6 jit_solution(17868271870395814350)
XLA Ops:
  0.6 32.5 %shard_map.68 = f32[4,2,4,4,8,128]{5,4,3,2,1,0:T(8,128)} custom-call(f32[2048,1024]{1,0:T(8,128)} %bitcast.3, f32[4,2,4,4,8,128]{5,4,3,2,1,0:T(8,128)} %bitcast.5, f32[8,128]{1,0:T(8,128)} %factor_two.1, f32[4,128]{1,0:T(4,128)} %factor_three.1, f32[64,128]{1,0:T(8,128)} %factor_four.1), custom_call_target="tpu_custom_call" | custom-call | tf_op jit(solution)/shard_map/pallas_call | solution.py:342
  33.1 2.5 %shard_map.69 = (f32[1024,128]{1,0:T(8,128)}, f32[128,128]{1,0:T(8,128)}) custom-call(f32[1024,128]{1,0:T(8,128)} %bitcast.4), custom_call_target="tpu_custom_call" | custom-call | tf_op jit(solution)/shard_map/pallas_call | solution.py:383
